TPU v7x, 32 devices: a whole 2x2x4 slice. The times are simulated.
32 devices in a mesh: plane: 4 (over z), mode: 8 (over y, x, core).
Axes of the slice: x: 2, y: 2, z: 4, core: 2. Of those that a mesh axis runs over, the one named last changes fastest.
Arguments:
- phase_masks: float32 [4, 512, 512], P('plane'), may hold values from -3.140625 to 3.140625
- hg_orders: int32 [32, 2], P('mode'), may hold values from 0 to 44
- spot_index: int32 [32], P('mode'), may hold values from 0 to 1023
Outputs:
- phase_next: float32 [4, 512, 512], P('plane')
Inputs may be any that keep to these rules, and one draw needn't show every extreme that they name: `spot_index`: the output spot of each mode; several modes may share a spot.
All inputs are finite; a program needn't handle non-finite values.
Results may differ from a plain program's by a relative error of at most 0.018.
Values may be sent and summed in bfloat16 or wider, within the bound.
A program may use at most 64 MiB of HBM per device.

v0:
```python
import math

import jax
import jax.numpy as jnp
from jax import lax
from jax.sharding import PartitionSpec as P

ORDERS = 45
SPOT_SIDE = 32


CHIRP_RATE = math.pi / 48.0 * (math.pi / 48.0)
AMPLITUDE = 12.0
EPSILON = 1e-06


def kernel_parts(extent):
    positions = jnp.arange(extent, dtype=jnp.int32)
    centred = (positions + extent // 2) % extent - extent // 2
    wrapped = positions[:, None] * positions[None, :] % extent
    chirp_phase = CHIRP_RATE * (centred * centred).astype(jnp.float32)
    angles = 2.0 * math.pi / extent * wrapped.astype(jnp.float32) - chirp_phase[None, :]
    kernel_re = jnp.sum(jnp.cos(angles), axis=1) / extent
    kernel_im = jnp.sum(jnp.sin(angles), axis=1) / extent
    return (kernel_re, kernel_im)


def circulant(values):
    extent = values.shape[0]
    repeated = jnp.tile(values, extent + 1)
    hankel = repeated.reshape(extent, extent + 1)[:, :extent]
    return jnp.roll(jnp.flip(hankel, 1), 1, 1)


def operators(extent):
    kernel_re, kernel_im = kernel_parts(extent)
    matrix_re = circulant(kernel_re)
    matrix_im = circulant(kernel_im)
    prop_re = matrix_re.astype(jnp.bfloat16)
    prop_im = matrix_im.astype(jnp.bfloat16)
    forward_mats = (prop_re, prop_im, (matrix_re + matrix_im).astype(jnp.bfloat16))
    backward_mats = (prop_re, -prop_im, (matrix_re - matrix_im).astype(jnp.bfloat16))
    return (forward_mats, backward_mats)


def left_product(left_re, left_im, left_sum, field_re, field_im):
    field_sum = (field_re.astype(jnp.float32) + field_im.astype(jnp.float32)).astype(jnp.bfloat16)
    first_term = jnp.dot(left_re, field_re, preferred_element_type=jnp.float32)
    second_term = jnp.dot(left_im, field_im, preferred_element_type=jnp.float32)
    third_term = jnp.dot(left_sum, field_sum, preferred_element_type=jnp.float32)
    return (first_term - second_term, third_term - first_term - second_term)


def right_product(field_re, field_im, right_re, right_im, right_sum):
    field_sum = (field_re.astype(jnp.float32) + field_im.astype(jnp.float32)).astype(jnp.bfloat16)
    first_term = jnp.dot(field_re, right_re, preferred_element_type=jnp.float32)
    second_term = jnp.dot(field_im, right_im, preferred_element_type=jnp.float32)
    third_term = jnp.dot(field_sum, right_sum, preferred_element_type=jnp.float32)
    return (first_term - second_term, third_term - first_term - second_term)


def propagate(field_re, field_im, matrices):
    matrix_re, matrix_im, matrix_sum = matrices
    middle_re, middle_im = left_product(matrix_re, matrix_im, matrix_sum, field_re, field_im)
    middle_re, middle_im = lax.optimization_barrier(
        (middle_re.astype(jnp.bfloat16), middle_im.astype(jnp.bfloat16))
    )
    return right_product(middle_re, middle_im, matrix_re, matrix_im, matrix_sum)


def hermite(orders, extent):
    scaled = (jnp.arange(extent, dtype=jnp.float32) - (extent - 1) / 2.0) / (extent / 48.0)
    lowest = math.pow(math.pi, -0.25) * jnp.exp(-0.5 * scaled * scaled)
    second = math.sqrt(2.0) * scaled * lowest
    chosen = jnp.where((orders == 0)[:, None], lowest[None, :], 0.0)
    chosen = jnp.where((orders == 1)[:, None], second[None, :], chosen)

    def advance(degree, carried):
        previous, current, picked = carried
        degree_f = degree.astype(jnp.float32)
        higher = (
            jnp.sqrt(2.0 / (degree_f + 1.0)) * scaled * current
            - jnp.sqrt(degree_f / (degree_f + 1.0)) * previous
        )
        picked = jnp.where((orders == degree + 1)[:, None], higher[None, :], picked)
        return (current, higher, picked)

    previous, current, chosen = lax.fori_loop(1, ORDERS - 1, advance, (lowest, second, chosen))
    return chosen


def spot_profile(spots, extent):
    coords = jnp.arange(extent, dtype=jnp.float32) - (extent - 1) / 2.0
    spacing = extent / 40.0
    spot_width = extent / 120.0
    centre = (SPOT_SIDE - 1) / 2.0
    spot_row = (spots // SPOT_SIDE).astype(jnp.float32) - centre
    spot_col = (spots % SPOT_SIDE).astype(jnp.float32) - centre
    offset_x = (coords[None, :] - spacing * spot_row[:, None]) / spot_width
    offset_y = (coords[None, :] - spacing * spot_col[:, None]) / spot_width
    return (jnp.exp(-offset_x * offset_x), jnp.exp(-offset_y * offset_y))


def mode_tables(orders, spots, extent):
    profile_x, profile_y = spot_profile(spots, extent)
    return (
        AMPLITUDE * hermite(orders[:, 0], extent),
        hermite(orders[:, 1], extent),
        profile_x,
        profile_y,
    )


def apply_mask(field_re, field_im, cos_mask, sin_mask):
    masked_re = (field_re * cos_mask - field_im * sin_mask).astype(jnp.bfloat16)
    masked_im = (field_re * sin_mask + field_im * cos_mask).astype(jnp.bfloat16)
    return lax.optimization_barrier((masked_re, masked_im))


def remove_mask(back_re, back_im, cos_mask, sin_mask):
    reply_re = (back_re * cos_mask + back_im * sin_mask).astype(jnp.bfloat16)
    reply_im = (back_im * cos_mask - back_re * sin_mask).astype(jnp.bfloat16)
    return lax.optimization_barrier((reply_re, reply_im))


def whole_mode(input_x, input_y, target, cos_masks, sin_masks, forward_mats, backward_mats):
    plane_count = cos_masks.shape[0]
    field_re = input_x[:, None] * input_y[None, :]
    field_im = jnp.zeros_like(field_re)
    masked_fields = []
    for plane_at in range(plane_count):
        masked_re, masked_im = apply_mask(
            field_re, field_im, cos_masks[plane_at], sin_masks[plane_at]
        )
        masked_fields.append((masked_re, masked_im))
        out_re, out_im = propagate(masked_re, masked_im, forward_mats)
        rounded = lax.optimization_barrier(
            (out_re.astype(jnp.bfloat16), out_im.astype(jnp.bfloat16))
        )
        field_re = rounded[0].astype(jnp.float32)
        field_im = rounded[1].astype(jnp.float32)
    coupling_re = jnp.sum(target * out_re)
    coupling_im = jnp.sum(target * out_im)
    source_re, source_im = lax.optimization_barrier(
        ((coupling_re * target).astype(jnp.bfloat16), (coupling_im * target).astype(jnp.bfloat16))
    )
    grad_terms = []
    for plane_at in reversed(range(plane_count)):
        back_re, back_im = propagate(source_re, source_im, backward_mats)
        masked_re, masked_im = masked_fields[plane_at]
        grad_terms.append(
            2.0
            * (back_im * masked_re.astype(jnp.float32) - back_re * masked_im.astype(jnp.float32))
        )
        source_re, source_im = remove_mask(
            back_re, back_im, cos_masks[plane_at], sin_masks[plane_at]
        )
    return jnp.stack(grad_terms[::-1])


def shards(phase_masks, hg_orders, spot_index):
    extent = phase_masks.shape[1]
    modes_here = hg_orders.shape[0]
    plane_count = lax.axis_size("plane")
    section_index = lax.axis_index("plane")
    forward_mats, backward_mats = operators(extent)
    all_masks = lax.all_gather(phase_masks, "plane", axis=0, tiled=True)
    cos_masks = jnp.cos(all_masks)
    sin_masks = jnp.sin(all_masks)
    per_section = modes_here // plane_count
    mode_start = section_index * per_section
    own_orders = lax.dynamic_slice_in_dim(hg_orders, mode_start, per_section, 0)
    own_spots = lax.dynamic_slice_in_dim(spot_index, mode_start, per_section, 0)
    own_tables = mode_tables(own_orders, own_spots, extent)

    def one_mode(mode_item, grad_total):
        picked_rows = [
            lax.dynamic_index_in_dim(entry_table, mode_item, 0, keepdims=False)
            for entry_table in own_tables
        ]
        target = picked_rows[2][:, None] * picked_rows[3][None, :]
        return grad_total + whole_mode(
            picked_rows[0],
            picked_rows[1],
            target,
            cos_masks,
            sin_masks,
            forward_mats,
            backward_mats,
        )

    grad_total = lax.fori_loop(
        0, per_section, one_mode, jnp.zeros((plane_count, extent, extent), jnp.float32)
    )
    local_sum = lax.psum_scatter(
        grad_total.astype(jnp.bfloat16), "plane", scatter_dimension=0, tiled=True
    ).astype(jnp.float32)[0]
    summed = lax.psum(local_sum, "mode")
    mean_square = jnp.mean(summed * summed)
    return (phase_masks[0] + summed / jnp.sqrt(mean_square + EPSILON))[None]


def solution(mesh):
    return jax.shard_map(
        shards,
        mesh=mesh,
        in_specs=(P("plane", None, None), P("mode", None), P("mode")),
        out_specs=P("plane", None, None),
        check_vma=False,
    )
```

profile of v0, /device:TPU:1, one launch (start us, length us, event | category | flops | bytes accessed | tf_op | source)
XLA Modules:
  0.0 270.2 jit_solution(5909438318516498454)
XLA Ops:
  6.5 0.7 all-gather.2.cloned.1.call-update
  7.4 0.6 fusion.112
  10.4 37.2 %while.45 = (s32[]{:T(128)}, f32[512]{0:T(512)S(1)}, f32[512]{0:T(512)S(1)}, f32[1,512]{1,0:T(1,128)S(1)}, s32[1]{0:T(128)}, /*index=5*/s32[]{:T(128)}, f32[]{:T(128)}, f32[]{:T(128)}, f32[]{:T(128)}, s32[]{:T(128)}) while((s32[]{:T(128)}, f32[512]{0:T(512)S(1)}, f32[512]{0:T(512)S(1)}, f32[1,512]{1,0:T(1,128)S(1)}, s32[1]{0:T(128)}, ...), condition=%wide.region_2.3_spmd.clone, body=%wide.region_1.2_spmd.clone.sunk | while | flops 3081 | bytes 20683 | solution.py:88
  47.7 34.3 %while.46 = (s32[]{:T(128)}, f32[512]{0:T(512)S(1)}, f32[512]{0:T(512)S(1)}, f32[1,512]{1,0:T(1,128)S(1)}, s32[1]{0:T(128)}, /*index=5*/s32[]{:T(128)}, f32[]{:T(128)}, f32[]{:T(128)}, f32[]{:T(128)}, s32[]{:T(128)}) while((s32[]{:T(128)}, f32[512]{0:T(512)S(1)}, f32[512]{0:T(512)S(1)}, f32[1,512]{1,0:T(1,128)S(1)}, s32[1]{0:T(128)}, ...), condition=%wide.region_4.5_spmd.clone, body=%wide.region_3.4_spmd.clone.sunk | while | flops 3081 | bytes 20683 | solution.py:88
  82.0 1.2 dynamic_slice.15
  85.8 5.0 %sine_reduce_fusion = (f32[512]{0:T(512)S(1)}, f32[512]{0:T(512)S(1)}) fusion(f32[512]{0:T(512)S(1)} %fusion.108), kind=kLoop, calls=%fused_computation.169 | loop fusion | flops 4455424 | bytes 6144 | tf_op jit(solution)/shard_map/reduce_sum | solution.py:24
  91.0 1.2 reshape_tile.7
  92.2 0.7 slice.92
  93.4 1.2 reshape_tile.6
  94.5 0.7 slice.88
  95.2 1.3 slice.89
  96.6 5.9 %reverse.5 = f32[512,512]{1,0:T(8,128)} reverse(f32[512,512]{1,0:T(8,128)S(1)} %bitcast.191), dimensions={1} | reverse | bytes 2097152
  102.5 1.6 slice.165
  104.0 1.5 reverse.4
  106.2 1.2 fusion.87
  107.4 0.6 subtract_convert_fusion.6
  108.1 16.0 %fusion.111 = (f32[4,512,512]{2,1,0:T(8,128)S(1)}, f32[4,512,512]{2,1,0:T(8,128)S(1)}) fusion(f32[4,512,512]{2,1,0:T(8,128)} %all-gather.2.cloned.1.call-done), kind=kLoop, calls=%fused_computation.223 | loop fusion | bytes 12582912 | tf_op jit(solution)/shard_map/sin | solution.py:169
  125.3 0.5 fusion.25
  126.7 0.4 fusion.26
  127.1 0.5 fusion.42
  128.5 0.5 fusion.27
  129.9 0.4 fusion.28
  130.3 0.5 fusion.50
  131.6 0.5 fusion.29
  133.0 0.4 fusion.30
  133.4 0.5 fusion.58
  134.8 0.5 fusion.31
  135.7 1.2 fusion.71
  136.9 1.3 fusion.78
  138.2 1.5 fusion.73
  140.5 0.5 fusion.32
  141.5 0.4 fusion.100
  141.9 0.9 subtract_convert_fusion.5
  143.7 0.5 fusion.33
  144.2 0.6 fusion.122
  144.8 0.4 fusion.96
  145.3 0.9 subtract_convert_fusion.3
  147.0 0.5 fusion.34
  148.4 0.9 subtract_convert_fusion.1
  150.2 0.5 fusion.35
  151.1 0.4 fusion.88
  151.6 0.7 fusion.37
  152.2 1.6 pad_maximum_fusion
  153.9 45.9 %reduce-scatter.2.cloned.1.call-done = bf16[1,512,512]{2,1,0:T(8,128)(2,1)} async-done(((bf16[4,512,512]{2,1,0:T(8,128)(2,1)}), bf16[1,512,512]{2,1,0:T(8,128)(2,1)}) %reduce-scatter.2.cloned.1.call-update) | async-done | bytes 524304 | tf_op jit(solution)/shard_map/reduce_scatter | solution.py:195
  199.8 2.1 bitcast_convert_fusion
  202.0 56.4 %all-reduce.2.cloned.1.call-done = f32[512,512]{1,0:T(8,128)} async-done(((f32[512,512]{1,0:T(8,128)}), f32[512,512]{1,0:T(8,128)}) %all-reduce.2.cloned.1.call-update) | async-done | bytes 1048592 | tf_op jit(solution)/shard_map/psum | solution.py:198
  258.4 2.1 multiply_reduce_fusion
  261.2 2.4 fusion.74
  (405 shorter events, 16.5 us)
Async XLA Ops:
  6.5 0.8 copy-start
  6.5 101.5 %all-gather.2.cloned.1.call-start = ((), (), s32[]{:S(2)}) async-start(), calls=%async_computation.1 | async-start | bytes 5242880 | tf_op jit(solution)/shard_map/all_gather | solution.py:167
  7.3 192.5 %reduce-scatter.2.cloned.1.call-start = ((), (), s32[]{:S(2)}) async-start(), calls=%async_computation.2 | async-start | bytes 2621440 | tf_op jit(solution)/shard_map/reduce_scatter | solution.py:195
  96.6 7.4 %copy-start.3 = (f32[512,511]{1,0:T(8,128)S(1)}, f32[512,511]{1,0:T(8,128)}, u32[]{:S(2)}) copy-start(f32[512,511]{1,0:T(8,128)} %slice.89) | copy-start | bytes 3139588
  96.6 9.3 %copy-start.4 = (f32[512,1]{1,0:T(8,128)S(1)}, f32[512,1]{1,0:T(8,128)}, u32[]{:S(2)}) copy-start(f32[512,1]{1,0:T(8,128)} %slice.92) | copy-start | bytes 6148
  105.5 1.9 copy-start.5
  152.2 108.9 %copy-start.2 = (f32[1,512,512]{2,1,0:T(8,128)S(1)}, f32[1,512,512]{2,1,0:T(8,128)}, u32[]{:S(2)}) copy-start(f32[1,512,512]{2,1,0:T(8,128)} %param.7) | copy-start | bytes 3145732
  153.8 109.8 %copy-start.1 = (s32[4,2]{0,1:T(2,128)S(1)}, s32[4,2]{0,1:T(2,128)}, u32[]{:S(2)}) copy-start(s32[4,2]{0,1:T(2,128)} %param.8) | copy-start | bytes 100
  153.9 104.5 %all-reduce.2.cloned.1.call-start = ((), (), s32[]{:S(2)}) async-start(), calls=%async_computation.3 | async-start | bytes 2097152 | tf_op jit(solution)/shard_map/psum | solution.py:198
Sparse Core Ops, SparseCore 0:
  8.9 82.8 all-gather.1
  154.0 45.7 reduce-scatter.1
  203.3 55.0 all-reduce.1
where the time goes:
time: 273 us; the launch traced here: 270 us
  waiting for transfers between devices  103 us (38%)
  loops' own time  68.7 us (25%)
  local copies, waits for them, and re-layouts  33.3 us (12%)
  matrix products  24.7 us (9%)
  other arithmetic  21.1 us (8%)
  between operations  19.3 us (7%)
    another operation x2, loops' own time, hermite(): lax.fori_loop(1, ORDERS - 1, advance, (lowest, second, chosen))  68.7 us
    psum x1, waiting for transfers between devices, shards(): summed = lax.psum(local_sum, 'mode')  56.4 us
    reduce_scatter x1, waiting for transfers between devices, shards(): lax.psum_scatter(grad_total.astype(jnp.bfloat16), 'plane', scatter_dimens...  45.9 us
    sin x1, local copies, waits for them, and re-layouts, shards(): sin_masks = jnp.sin(all_masks)  16 us
    unnamed x18, local copies, waits for them, and re-layouts  9.31 us
    dot_general x8, matrix products, right_product(): jnp.dot(field_sum, right_sum, preferred_element_type=jnp.float32)  5.85 us
  transfers between devices with their start and end apart: 3, of which 2 were waited for; matrix products, arithmetic and copies ran while one was open for 10% of the time, Pallas kernels for 0%

commit v1 on v0

v1 whole, which is shorter than its diff:
```python
import functools
import math

import jax
import jax.numpy as jnp
from jax import lax
from jax.experimental import pallas as pl
from jax.experimental.pallas import tpu as pltpu
from jax.sharding import PartitionSpec as P

ORDERS = 45
SPOT_SIDE = 32
CHIRP_RATE = math.pi / 48.0 * (math.pi / 48.0)
AMPLITUDE = 12.0
EPSILON = 1e-06
CODE = 26.0
CHUNK = 16
F32 = jnp.float32
BF16 = jnp.bfloat16
MESH = pl.DeviceIdType.MESH

SIN_HALF = [(-1.0) ** n / math.factorial(2 * n + 1) for n in range(6)]
COS_HALF = [(-1.0) ** n / math.factorial(2 * n) for n in range(6)]


def horner(u, coefficients):
    total = jnp.full_like(u, coefficients[-1])
    for value in coefficients[-2::-1]:
        total = total * u + value
    return total


def sincos(x):
    h = 0.5 * x
    u = h * h
    s = h * horner(u, SIN_HALF)
    c = horner(u, COS_HALF)
    return 2.0 * s * c, 1.0 - 2.0 * s * s


def exact_dot(a, b, contract):
    return lax.dot_general(
        a, b, ((contract[:1], contract[1:]), ((), ())),
        precision=lax.Precision.HIGHEST, preferred_element_type=F32,
    )


def make_operators(n, left_ref, right_ref, prop_ref):
    h = n // 2
    rows = lax.broadcasted_iota(jnp.int32, (h, h), 0)
    slots = lax.broadcasted_iota(jnp.int32, (h, h), 1)
    for a in range(2):
        freq = 2 * slots + a
        turn = ((freq * rows + h) & (n - 1)) - h
        s, c = sincos(turn.astype(F32) * (2.0 * math.pi / n))
        basis = jnp.concatenate([c, s], axis=1)
        freq_row = 2 * lax.broadcasted_iota(jnp.int32, (8, h), 1) + a
        centred = ((freq_row + h) & (n - 1)) - h
        turns = (centred * centred).astype(F32) * (CHIRP_RATE / (2.0 * math.pi))
        turns = turns - jnp.floor(turns + 0.5)
        chirp_s, chirp_c = sincos(turns * (2.0 * math.pi))
        for part, weight in enumerate((chirp_c, -chirp_s)):
            weight = weight[:1] * (1.0 / n)
            weighted = basis * jnp.concatenate([weight, weight], axis=1)
            prop_ref[a, part] = exact_dot(weighted, basis, (1, 1))
        re, im = prop_ref[a, 0].astype(BF16), prop_ref[a, 1].astype(BF16)
        left_ref[a, :h, :h] = re
        left_ref[a, :h, h:] = -im
        left_ref[a, h:, :h] = im
        left_ref[a, h:, h:] = re
        right_ref[a, :h, :h] = re
        right_ref[a, :h, h:] = im
        right_ref[a, h:, :h] = -im
        right_ref[a, h:, h:] = re


def make_tables(n, order_x, order_y, spot, prop_ref, row_ref, col_ref):
    h = n // 2
    coords = lax.broadcasted_iota(jnp.int32, (8, n), 1).astype(F32) - (n - 1) / 2.0
    row_id = lax.broadcasted_iota(jnp.int32, (8, n), 0)
    orders = jnp.where(row_id == 0, order_x, order_y)
    scaled = coords * (48.0 / n)
    previous = math.pow(math.pi, -0.25) * jnp.exp(-0.5 * scaled * scaled)
    current = math.sqrt(2.0) * scaled * previous
    picked = jnp.where(orders == 0, previous, current)
    for degree in range(1, ORDERS - 1):
        higher = (
            math.sqrt(2.0 / (degree + 1.0)) * scaled * current
            - math.sqrt(degree / (degree + 1.0)) * previous
        )
        picked = jnp.where(orders == degree + 1, higher, picked)
        previous, current = current, higher
    centre = (SPOT_SIDE - 1) / 2.0
    spot_row = (spot // SPOT_SIDE).astype(F32) - centre
    spot_col = (spot % SPOT_SIDE).astype(F32) - centre
    place = jnp.where(row_id == 0, spot_row, spot_col)
    offset = (coords - (n / 40.0) * place) * (120.0 / n)
    profile = jnp.exp(-offset * offset)
    spread = []
    for part in range(2):
        s = exact_dot(profile[:, :h] + profile[:, h:], prop_ref[0, part], (1, 0))
        d = exact_dot(profile[:, :h] - profile[:, h:], prop_ref[1, part], (1, 0))
        spread.append(jnp.concatenate([s + d, s - d], axis=1))
    table = jnp.concatenate(
        [
            AMPLITUDE * picked[0:1], picked[1:2],
            spread[0][0:1], spread[1][0:1], spread[0][1:2], spread[1][1:2],
            jnp.zeros((2, n), F32),
        ],
        axis=0,
    )
    row_ref[...] = table
    wide = jnp.concatenate([table, jnp.zeros((120, n), F32)], axis=0)
    col_ref[...] = wide.T


def kernel(
    planes, modes, orders_ref, spots_ref, mask_ref, out_ref,
    code, cosm, sinm, g_re, g_im, x_buf, w_buf, y_buf, left, right, prop, row_tab, col_tab,
    grad, in_a, sum_a, in_b, piece, in_c, final,
    mz_s, mz_r, ml_s, ml_r, mc_s, mc_r, a_s, a_r, b_s, b_r, c_s, c_r, d_s, d_r, e_s, e_r,
):
    n = mask_ref.shape[-1]
    h = n // 2
    chips = modes // 2
    rows = n // chips
    p = lax.axis_index("plane")
    m = lax.axis_index("mode")
    core = m % 2
    chip = m // 2
    partner = m + 1 - 2 * core

    def at_chip(step):
        return (chip + step) % chips

    def rows_of(which):
        return pl.ds(pl.multiple_of(which * rows, rows), rows)

    def remote(src, dst, send, recv, plane=None, mode=None):
        return pltpu.make_async_remote_copy(
            src_ref=src, dst_ref=dst, send_sem=send, recv_sem=recv,
            device_id=(p if plane is None else plane, m if mode is None else mode),
            device_id_type=MESH,
        )

    mine = rows_of(chip)

    def mask_z(step):
        spot = code.at[p, core, mine]
        return remote(spot, spot, mz_s.at[step - 1], mz_r.at[p], plane=(p + step) % planes)

    def mask_z_in(k):
        spot = code.at[k, core, mine]
        return remote(spot, spot, mz_s.at[0], mz_r.at[k], plane=(p + 1) % planes)

    def mask_layer(k, step):
        spot = code.at[k, core, mine]
        return remote(
            spot, spot, ml_s.at[k, step - 1], ml_r.at[k, step - 1], mode=at_chip(step) * 2 + core
        )

    def mask_core(k):
        return remote(code.at[k, core], code.at[k, core], mc_s.at[k], mc_r.at[k], mode=partner)

    def grad_a(k):
        return remote(grad.at[k, 1 - core], in_a.at[k], a_s.at[k], a_r.at[k], mode=partner)

    def grad_b(k, step):
        there = at_chip(step)
        return remote(
            sum_a.at[k, rows_of(there)], in_b.at[k, step - 1], b_s.at[k, step - 1],
            b_r.at[k, step - 1], mode=there * 2 + core,
        )

    def grad_c(k):
        return remote(piece.at[k], in_c.at[p], c_s.at[k], c_r.at[p], plane=k)

    def grad_c_in(source):
        return remote(piece.at[0], in_c.at[source], c_s.at[0], c_r.at[source], plane=source)

    def grad_d(step):
        spot = final.at[core, mine]
        return remote(
            spot, spot, d_s.at[step - 1], d_r.at[step - 1], mode=at_chip(step) * 2 + core
        )

    def grad_e():
        return remote(final.at[core], final.at[core], e_s.at[0], e_r.at[0], mode=partner)

    barrier = pltpu.get_barrier_semaphore()
    for step in range(1, planes):
        pl.semaphore_signal(
            barrier, inc=1, device_id=((p + step) % planes, m), device_id_type=MESH
        )
    for step in range(1, chips):
        pl.semaphore_signal(
            barrier, inc=1, device_id=(p, at_chip(step) * 2 + core), device_id_type=MESH
        )
    pl.semaphore_signal(barrier, inc=1, device_id=(p, partner), device_id_type=MESH)

    for b in range(2):
        code[p, b] = jnp.exp(CODE * mask_ref[0, :, b * h : (b + 1) * h]).astype(BF16)
    pl.semaphore_wait(barrier, planes - 1 + chips - 1 + 1)

    for step in range(1, planes):
        mask_z(step).start()

    make_operators(n, left, right, prop)

    for k in range(planes):
        @pl.when(p != k)
        def _():
            mask_z_in(k).wait_recv()
            for step in range(1, chips):
                mask_layer(k, step).start()

    make_tables(n, orders_ref[p, 0], orders_ref[p, 1], spots_ref[p], prop, row_tab, col_tab)

    quads = [(a, b) for a in range(2) for b in range(2)]

    def span(i, a):
        return pl.ds(pl.multiple_of(a * h + i * CHUNK, CHUNK), CHUNK)

    def hadamard(q):
        top, bottom = q[0, 0] + q[0, 1], q[1, 0] + q[1, 1]
        top_d, bottom_d = q[0, 0] - q[0, 1], q[1, 0] - q[1, 1]
        return {
            (0, 0): top + bottom, (0, 1): top_d + bottom_d,
            (1, 0): top - bottom, (1, 1): top_d - bottom_d,
        }

    def combined(i):
        re = hadamard({(a, b): y_buf[b, span(i, a), :h] for a, b in quads})
        im = hadamard({(a, b): y_buf[b, span(i, a), h:] for a, b in quads})
        return re, im

    def put_sums(i, re, im):
        for part, q in enumerate((hadamard(re), hadamard(im))):
            for a, b in quads:
                x_buf[a, span(i, part), b * h : (b + 1) * h] = q[a, b].astype(BF16)

    def products(first, second):
        for a in range(2):
            v = jnp.dot(first[a], x_buf[a], preferred_element_type=F32)
            for b in range(2):
                for part in range(2):
                    w_buf[b, a * h : (a + 1) * h, part * h : (part + 1) * h] = v[
                        part * h : (part + 1) * h, b * h : (b + 1) * h
                    ].astype(BF16)
        for b in range(2):
            y_buf[b] = jnp.dot(w_buf[b], second[b], preferred_element_type=F32)

    def outer(i, a, b):
        ar, ai = col_tab[span(i, a), 2:3], col_tab[span(i, a), 3:4]
        br, bi = row_tab[4:5, b * h : (b + 1) * h], row_tab[5:6, b * h : (b + 1) * h]
        return ar * br - ai * bi, ar * bi + ai * br

    for k in range(planes):
        @pl.when(p != k)
        def _():
            for step in range(1, chips):
                mask_layer(k, step).wait_recv()
            mask_core(k).start()
            mask_core(k).wait_recv()

        last = k == planes - 1

        def forward(i, carry):
            if k == 0:
                field_re = {
                    (a, b): col_tab[span(i, a), 0:1] * row_tab[1:2, b * h : (b + 1) * h]
                    for a, b in quads
                }
                field_im = None
            else:
                field_re, field_im = combined(i)
            masked_re, masked_im = {}, {}
            for a, b in quads:
                phase = jnp.log(code[k, b, span(i, a)].astype(F32)) * (1.0 / CODE)
                s, c = sincos(phase)
                cosm[k, b, span(i, a)] = c
                sinm[k, b, span(i, a)] = s
                if field_im is None:
                    re, im = field_re[a, b] * c, field_re[a, b] * s
                else:
                    fr, fi = field_re[a, b], field_im[a, b]
                    re, im = fr * c - fi * s, fr * s + fi * c
                masked_re[a, b], masked_im[a, b] = re, im
                g_re[k, b, span(i, a)] = re.astype(BF16)
                g_im[k, b, span(i, a)] = im.astype(BF16)
            if not last:
                put_sums(i, masked_re, masked_im)
                return carry
            total_re, total_im = carry
            for a, b in quads:
                er, ei = outer(i, a, b)
                re, im = masked_re[a, b], masked_im[a, b]
                total_re += er * re - ei * im
                total_im += er * im + ei * re
            return total_re, total_im

        zero = jnp.zeros((CHUNK, h), F32)
        totals = lax.fori_loop(0, h // CHUNK, forward, (zero, zero) if last else 0)
        if not last:
            products(left, right)
    coupling_re = jnp.sum(totals[0], keepdims=True)
    coupling_im = jnp.sum(totals[1], keepdims=True)

    def settle_a(k):
        grad_a(k).wait_recv()
        sum_a[k] = (grad[k, core].astype(F32) + in_a[k].astype(F32)).astype(BF16)
        for step in range(1, chips):
            grad_b(k, step).start()

    def settle_b(k):
        for step in range(1, chips):
            grad_b(k, step).wait_recv()
        total = sum_a[k, mine].astype(F32)
        for step in range(1, chips):
            total += in_b[k, step - 1].astype(F32)
        piece[k] = total.astype(BF16)

        @pl.when(p != k)
        def _():
            grad_c(k).start()

        @pl.when(p == k)
        def _():
            in_c[k] = piece[k]

    for k in range(planes - 1, -1, -1):
        def backward(i, carry):
            if k == planes - 1:
                back_re, back_im = {}, {}
                for a, b in quads:
                    er, ei = outer(i, a, b)
                    back_re[a, b] = coupling_re * er + coupling_im * ei
                    back_im[a, b] = coupling_im * er - coupling_re * ei
            else:
                back_re, back_im = combined(i)
            reply_re, reply_im = {}, {}
            for a, b in quads:
                br, bi = back_re[a, b], back_im[a, b]
                gr = g_re[k, b, span(i, a)].astype(F32)
                gi = g_im[k, b, span(i, a)].astype(F32)
                grad[k, b, span(i, a)] = (2.0 * (bi * gr - br * gi)).astype(BF16)
                if k > 0:
                    c, s = cosm[k, b, span(i, a)], sinm[k, b, span(i, a)]
                    reply_re[a, b] = br * c + bi * s
                    reply_im[a, b] = bi * c - br * s
            if k > 0:
                put_sums(i, reply_re, reply_im)
            return carry

        lax.fori_loop(0, h // CHUNK, backward, 0)
        grad_a(k).start()
        if k + 2 < planes:
            settle_b(k + 2)
        if k + 1 < planes:
            settle_a(k + 1)
        if k > 0:
            products(right, left)
    settle_a(0)
    if planes > 1:
        settle_b(1)
    settle_b(0)

    for k in range(planes):
        @pl.when(p != k)
        def _():
            grad_c_in(k).wait_recv()
    total = in_c[0].astype(F32)
    for k in range(1, planes):
        total += in_c[k].astype(F32)
    final[core, mine] = total.astype(BF16)
    for step in range(1, chips):
        grad_d(step).start()
    for step in range(1, chips):
        grad_d(step).wait_recv()
    grad_e().start()
    grad_e().wait_recv()

    def square(i, carry):
        here = pl.ds(pl.multiple_of(i * CHUNK, CHUNK), CHUNK)
        for b in range(2):
            g = final[b, here].astype(F32)
            carry += g * g
        return carry

    squares = lax.fori_loop(0, n // CHUNK, square, jnp.zeros((CHUNK, h), F32))
    mean_square = jnp.sum(squares, keepdims=True) * (1.0 / (n * n))
    scale = 1.0 / jnp.sqrt(mean_square + EPSILON)

    def finish(i, carry):
        here = pl.ds(pl.multiple_of(i * CHUNK, CHUNK), CHUNK)
        for b in range(2):
            cols = slice(b * h, (b + 1) * h)
            out_ref[0, here, cols] = mask_ref[0, here, cols] + final[b, here].astype(F32) * scale
        return carry

    lax.fori_loop(0, n // CHUNK, finish, 0)

    for step in range(1, planes):
        mask_z(step).wait_send()
    for k in range(planes):
        @pl.when(p != k)
        def _():
            for step in range(1, chips):
                mask_layer(k, step).wait_send()
            mask_core(k).wait_send()
            grad_c(k).wait_send()

        grad_a(k).wait_send()
        for step in range(1, chips):
            grad_b(k, step).wait_send()
    for step in range(1, chips):
        grad_d(step).wait_send()
    grad_e().wait_send()


def shards(planes, modes, phase_masks, hg_orders, spot_index):
    n = phase_masks.shape[1]
    h = n // 2
    chips = modes // 2
    rows = n // chips
    others = max(chips - 1, 1)
    assert hg_orders.shape[0] == planes and n & (n - 1) == 0
    dma = pltpu.SemaphoreType.DMA
    vmem = pltpu.VMEM
    return pl.pallas_call(
        functools.partial(kernel, planes, modes),
        out_shape=jax.ShapeDtypeStruct((1, n, n), F32),
        in_specs=[
            pl.BlockSpec(memory_space=pltpu.SMEM),
            pl.BlockSpec(memory_space=pltpu.SMEM),
            pl.BlockSpec(memory_space=pltpu.VMEM),
        ],
        out_specs=pl.BlockSpec(memory_space=pltpu.VMEM),
        scratch_shapes=[
            vmem((planes, 2, n, h), BF16),
            vmem((planes, 2, n, h), F32),
            vmem((planes, 2, n, h), F32),
            vmem((planes, 2, n, h), BF16),
            vmem((planes, 2, n, h), BF16),
            vmem((2, n, n), BF16),
            vmem((2, n, n), BF16),
            vmem((2, n, n), F32),
            vmem((2, n, n), BF16),
            vmem((2, n, n), BF16),
            vmem((2, 2, h, h), F32),
            vmem((8, n), F32),
            vmem((n, 128), F32),
            vmem((planes, 2, n, h), BF16),
            vmem((planes, n, h), BF16),
            vmem((planes, n, h), BF16),
            vmem((planes, others, rows, h), BF16),
            vmem((planes, rows, h), BF16),
            vmem((planes, rows, h), BF16),
            vmem((2, n, h), BF16),
            dma((max(planes - 1, 1),)), dma((planes,)),
            dma((planes, others)), dma((planes, others)),
            dma((planes,)), dma((planes,)),
            dma((planes,)), dma((planes,)),
            dma((planes, others)), dma((planes, others)),
            dma((planes,)), dma((planes,)),
            dma((others,)), dma((others,)),
            dma((1,)), dma((1,)),
        ],
        compiler_params=pltpu.CompilerParams(
            collective_id=0, has_side_effects=True, vmem_limit_bytes=52 * 1024 * 1024
        ),
        name="phase_update",
    )(hg_orders, spot_index, phase_masks)


def solution(mesh):
    planes, modes = mesh.shape["plane"], mesh.shape["mode"]
    return jax.shard_map(
        functools.partial(shards, planes, modes),
        mesh=mesh,
        in_specs=(P("plane", None, None), P("mode", None), P("mode")),
        out_specs=P("plane", None, None),
        check_vma=False,
    )
```

time: 273 us -> 70.2 us (0.26)
  waiting for transfers between devices: 103 us -> 0 us
  loops' own time: 68.7 us -> 0 us
  Pallas kernels: 0 us -> 68.3 us
  local copies, waits for them, and re-layouts: 33.3 us -> 1.75 us
  matrix products: 24.7 us -> 0 us
  other arithmetic: 21.1 us -> 0 us
  between operations: 19.3 us -> 0.01 us
    another operation x2 -> x0, loops' own time: 68.7 us -> none  [hermite(): lax.fori_loop(1, ORDERS - 1, advance, (lowest, second, chosen))]
    pallas_call x0 -> x1, Pallas kernels: none -> 68.3 us  [shards(): pl.pallas_call(functools.partial(kernel, planes, modes), out_shape=jax.Sh...]
    psum x1 -> x0, waiting for transfers between devices: 56.4 us -> none  [shards(): summed = lax.psum(local_sum, 'mode')]
    reduce_scatter x1 -> x0, waiting for transfers between devices: 45.9 us -> none  [shards(): lax.psum_scatter(grad_total.astype(jnp.bfloat16), 'plane', scatter_dimens...]
    dot_general x48 -> x0, matrix products: 24.7 us -> none  [the longest x8 5.85 us: right_product(): jnp.dot(field_sum, right_sum, preferred_element_type=jnp.float32)]
    sin x1 -> x0, local copies, waits for them, and re-layouts: 16 us -> none  [shards(): sin_masks = jnp.sin(all_masks)]
    unnamed x18 -> x4, local copies, waits for them, and re-layouts: 9.31 us -> 1.75 us
    reduce_sum x2 -> x0, other arithmetic: 7.13 us -> none  [the longest x1 5.03 us: kernel_parts(): kernel_im = jnp.sum(jnp.sin(angles), axis=1) / extent]
  transfers between devices with their start and end apart: 3 -> 0, of which waited for: 2 -> 0; matrix products, arithmetic and copies ran while one was open for 10% -> 0% of each run, Pallas kernels for 0% -> 0%
where the time goes in v1:
time: 70.2 us; the launch traced here: 70.1 us
  Pallas kernels  68.3 us (97%)
  local copies, waits for them, and re-layouts  1.75 us (2%)
    pallas_call x1, Pallas kernels, shards(): pl.pallas_call(functools.partial(kernel, planes, modes), out_shape=jax.Sh...  68.3 us
    unnamed x4, local copies, waits for them, and re-layouts  1.75 us

profile of v1, /device:TPU:1, one launch (start us, length us, event | category | flops | bytes accessed | tf_op | source)
XLA Modules:
  0.0 70.1 jit_solution(11321926247177081089)
XLA Ops:
  0.0 0.0 copy-start
  0.0 0.8 %copy.4.orders_ref = s32[4,2]{1,0:T(4,128)S(1)} copy(s32[4,2]{0,1:T(2,128)} %param.4) | data formatting | bytes 64 | tf_op args[1]
  0.8 0.0 copy-done
  0.8 68.3 %phase_update.1 = f32[1,512,512]{2,1,0:T(8,128)S(1)} custom-call(s32[4,2]{1,0:T(4,128)S(1)} %copy.4.orders_ref, s32[4]{0:T(128)S(1)} %copy-done, f32[1,512,512]{2,1,0:T(8,128)} %mask_ref.1), custom_call_target="tpu_custom_call" | custom-call | tf_op jit(solution)/shard_map/phase_update/pallas_call | solution.py:430
  69.1 1.0 %copy.6 = f32[1,512,512]{2,1,0:T(8,128)} copy(f32[1,512,512]{2,1,0:T(8,128)S(1)} %phase_update.1) | data formatting | bytes 2097152
Async XLA Ops:
  0.0 0.8 %copy-start = (s32[4]{0:T(128)S(1)}, s32[4]{0:T(128)}, u32[]{:S(2)}) copy-start(s32[4]{0:T(128)} %spots_ref.1) | copy-start | bytes 52

commit v2 on v1

--- a/solution.py
+++ b/solution.py
@@ -184,8 +184,9 @@
             spot, spot, d_s.at[step - 1], d_r.at[step - 1], mode=at_chip(step) * 2 + core
         )
 
-    def grad_e():
-        return remote(final.at[core], final.at[core], e_s.at[0], e_r.at[0], mode=partner)
+    def grad_e(step):
+        spot = final.at[core, rows_of(at_chip(chips - step))]
+        return remote(spot, spot, e_s.at[step], e_r.at[step], mode=partner)
 
     barrier = pltpu.get_barrier_semaphore()
     for step in range(1, planes):
@@ -207,14 +208,27 @@
 
     make_operators(n, left, right, prop)
 
-    for k in range(planes):
+    def spread_layer(k):
         @pl.when(p != k)
         def _():
             mask_z_in(k).wait_recv()
             for step in range(1, chips):
                 mask_layer(k, step).start()
 
-    make_tables(n, orders_ref[p, 0], orders_ref[p, 1], spots_ref[p], prop, row_tab, col_tab)
+    def spread_core(k):
+        @pl.when(p != k)
+        def _():
+            for step in range(1, chips):
+                mask_layer(k, step).wait_recv()
+            mask_core(k).start()
+
+    for k in range(min(2, planes)):
+        spread_layer(k)
+
+    make_tables(
+        n, orders_ref[0, p], orders_ref[1, p], spots_ref[p], prop, row_tab, col_tab
+    )
+    spread_core(0)
 
     quads = [(a, b) for a in range(2) for b in range(2)]
 
@@ -258,11 +272,10 @@
     for k in range(planes):
         @pl.when(p != k)
         def _():
-            for step in range(1, chips):
-                mask_layer(k, step).wait_recv()
-            mask_core(k).start()
             mask_core(k).wait_recv()
 
+        if k + 2 < planes:
+            spread_layer(k + 2)
         last = k == planes - 1
 
         def forward(i, carry):
@@ -302,6 +315,7 @@
         zero = jnp.zeros((CHUNK, h), F32)
         totals = lax.fori_loop(0, h // CHUNK, forward, (zero, zero) if last else 0)
         if not last:
+            spread_core(k + 1)
             products(left, right)
     coupling_re = jnp.sum(totals[0], keepdims=True)
     coupling_im = jnp.sum(totals[1], keepdims=True)
@@ -354,15 +368,11 @@
 
         lax.fori_loop(0, h // CHUNK, backward, 0)
         grad_a(k).start()
-        if k + 2 < planes:
-            settle_b(k + 2)
-        if k + 1 < planes:
-            settle_a(k + 1)
         if k > 0:
             products(right, left)
-    settle_a(0)
-    if planes > 1:
-        settle_b(1)
+        if k + 1 < planes:
+            settle_b(k + 1)
+        settle_a(k)
     settle_b(0)
 
     for k in range(planes):
@@ -375,10 +385,12 @@
     final[core, mine] = total.astype(BF16)
     for step in range(1, chips):
         grad_d(step).start()
+    grad_e(0).start()
     for step in range(1, chips):
         grad_d(step).wait_recv()
-    grad_e().start()
-    grad_e().wait_recv()
+        grad_e(step).start()
+    for step in range(chips):
+        grad_e(step).wait_recv()
 
     def square(i, carry):
         here = pl.ds(pl.multiple_of(i * CHUNK, CHUNK), CHUNK)
@@ -415,7 +427,8 @@
             grad_b(k, step).wait_send()
     for step in range(1, chips):
         grad_d(step).wait_send()
-    grad_e().wait_send()
+    for step in range(chips):
+        grad_e(step).wait_send()
 
 
 def shards(planes, modes, phase_masks, hg_orders, spot_index):
@@ -464,13 +477,13 @@
             dma((planes, others)), dma((planes, others)),
             dma((planes,)), dma((planes,)),
             dma((others,)), dma((others,)),
-            dma((1,)), dma((1,)),
+            dma((chips,)), dma((chips,)),
         ],
         compiler_params=pltpu.CompilerParams(
             collective_id=0, has_side_effects=True, vmem_limit_bytes=52 * 1024 * 1024
         ),
         name="phase_update",
-    )(hg_orders, spot_index, phase_masks)
+    )(hg_orders.T, spot_index, phase_masks)
 
 
 def solution(mesh):

time: 70.2 us -> 67.2 us (0.957)
  Pallas kernels: 68.3 us -> 65.4 us
    pallas_call x1, Pallas kernels: 68.3 us -> 65.4 us  [shards(): pl.pallas_call(functools.partial(kernel, planes, modes), out_shape=jax.Sh...]
    unnamed x4 -> x5, local copies, waits for them, and re-layouts: 1.75 us -> 1.67 us
where the time goes in v2:
time: 67.2 us; the launch traced here: 67.1 us
  Pallas kernels  65.4 us (97%)
  local copies, waits for them, and re-layouts  1.67 us (2%)
    pallas_call x1, Pallas kernels, shards(): pl.pallas_call(functools.partial(kernel, planes, modes), out_shape=jax.Sh...  65.4 us
    unnamed x5, local copies, waits for them, and re-layouts  1.67 us

profile of v2, /device:TPU:1, one launch (start us, length us, event | category | flops | bytes accessed | tf_op | source)
XLA Modules:
  0.0 67.1 jit_solution(13905753645988789771)
XLA Ops:
  0.0 0.0 copy-start.1
  0.0 0.0 copy-start
  0.0 0.7 copy-done.1
  0.7 0.0 copy-done
  0.7 65.4 %phase_update.1 = f32[1,512,512]{2,1,0:T(8,128)S(1)} custom-call(s32[2,4]{1,0:T(2,128)S(1)} %bitcast.1, s32[4]{0:T(128)S(1)} %copy-done.1, f32[1,512,512]{2,1,0:T(8,128)} %mask_ref.1), custom_call_target="tpu_custom_call" | custom-call | tf_op jit(solution)/shard_map/phase_update/pallas_call | solution.py:443
  66.1 1.0 %copy.5 = f32[1,512,512]{2,1,0:T(8,128)} copy(f32[1,512,512]{2,1,0:T(8,128)S(1)} %phase_update.1) | data formatting | bytes 2097152
Async XLA Ops:
  0.0 0.7 copy-start.1
  0.0 0.7 %copy-start = (s32[4,2]{0,1:T(2,128)S(1)}, s32[4,2]{0,1:T(2,128)}, u32[]{:S(2)}) copy-start(s32[4,2]{0,1:T(2,128)} %param.4) | copy-start | bytes 100

commit v3 on v2

--- a/solution.py
+++ b/solution.py
@@ -13,7 +13,6 @@
 CHIRP_RATE = math.pi / 48.0 * (math.pi / 48.0)
 AMPLITUDE = 12.0
 EPSILON = 1e-06
-CODE = 26.0
 CHUNK = 16
 F32 = jnp.float32
 BF16 = jnp.bfloat16
@@ -38,14 +37,26 @@
     return 2.0 * s * c, 1.0 - 2.0 * s * s
 
 
-def exact_dot(a, b, contract):
-    return lax.dot_general(
-        a, b, ((contract[:1], contract[1:]), ((), ())),
-        precision=lax.Precision.HIGHEST, preferred_element_type=F32,
-    )
-
-
-def make_operators(n, left_ref, right_ref, prop_ref):
+def quarter_tan(x):
+    h = 0.5 * x
+    u = h * h
+    return h * horner(u, SIN_HALF) / (1.0 + horner(u, COS_HALF))
+
+
+def sincos_of(t):
+    twice = 2.0 / (1.0 + t * t)
+    half_cos = twice - 1.0
+    half_sin = t * twice
+    double = 2.0 * half_sin
+    return double * half_cos, 1.0 - double * half_sin
+
+
+def split(x):
+    high = x.astype(BF16)
+    return high, (x - high.astype(F32)).astype(BF16)
+
+
+def make_operators(n, left_ref, right_ref):
     h = n // 2
     rows = lax.broadcasted_iota(jnp.int32, (h, h), 0)
     slots = lax.broadcasted_iota(jnp.int32, (h, h), 1)
@@ -59,11 +70,18 @@
         turns = (centred * centred).astype(F32) * (CHIRP_RATE / (2.0 * math.pi))
         turns = turns - jnp.floor(turns + 0.5)
         chirp_s, chirp_c = sincos(turns * (2.0 * math.pi))
-        for part, weight in enumerate((chirp_c, -chirp_s)):
+        weighted = []
+        for weight in (chirp_c, -chirp_s):
             weight = weight[:1] * (1.0 / n)
-            weighted = basis * jnp.concatenate([weight, weight], axis=1)
-            prop_ref[a, part] = exact_dot(weighted, basis, (1, 1))
-        re, im = prop_ref[a, 0].astype(BF16), prop_ref[a, 1].astype(BF16)
+            weighted.append(basis * jnp.concatenate([weight, weight], axis=1))
+        high, low = split(jnp.concatenate(weighted, axis=0))
+        basis_high, basis_low = split(basis)
+        prop = lax.dot_general(
+            jnp.concatenate([high, high, low], axis=1),
+            jnp.concatenate([basis_high, basis_low, basis_high], axis=1),
+            (((1,), (1,)), ((), ())), preferred_element_type=F32,
+        ).astype(BF16)
+        re, im = prop[:h], prop[h:]
         left_ref[a, :h, :h] = re
         left_ref[a, :h, h:] = -im
         left_ref[a, h:, :h] = im
@@ -74,7 +92,7 @@
         right_ref[a, h:, h:] = re
 
 
-def make_tables(n, order_x, order_y, spot, prop_ref, row_ref, col_ref):
+def make_tables(n, order_x, order_y, spot, right_ref, row_ref, col_ref):
     h = n // 2
     coords = lax.broadcasted_iota(jnp.int32, (8, n), 1).astype(F32) - (n - 1) / 2.0
     row_id = lax.broadcasted_iota(jnp.int32, (8, n), 0)
@@ -96,10 +114,18 @@
     place = jnp.where(row_id == 0, spot_row, spot_col)
     offset = (coords - (n / 40.0) * place) * (120.0 / n)
     profile = jnp.exp(-offset * offset)
+    halves = []
+    for a, folded in enumerate(
+        (profile[:, :h] + profile[:, h:], profile[:, :h] - profile[:, h:])
+    ):
+        high, low = split(folded)
+        both = jnp.dot(
+            jnp.concatenate([high, low], axis=0), right_ref[a, :h], preferred_element_type=F32
+        )
+        halves.append(both[:8] + both[8:])
     spread = []
     for part in range(2):
-        s = exact_dot(profile[:, :h] + profile[:, h:], prop_ref[0, part], (1, 0))
-        d = exact_dot(profile[:, :h] - profile[:, h:], prop_ref[1, part], (1, 0))
+        s, d = (half[:, part * h : (part + 1) * h] for half in halves)
         spread.append(jnp.concatenate([s + d, s - d], axis=1))
     table = jnp.concatenate(
         [
@@ -116,7 +142,7 @@
 
 def kernel(
     planes, modes, orders_ref, spots_ref, mask_ref, out_ref,
-    code, cosm, sinm, g_re, g_im, x_buf, w_buf, y_buf, left, right, prop, row_tab, col_tab,
+    code, cosm, sinm, g_re, g_im, x_buf, w_buf, y_buf, left, right, row_tab, col_tab,
     grad, in_a, sum_a, in_b, piece, in_c, final,
     mz_s, mz_r, ml_s, ml_r, mc_s, mc_r, a_s, a_r, b_s, b_r, c_s, c_r, d_s, d_r, e_s, e_r,
 ):
@@ -199,14 +225,22 @@
         )
     pl.semaphore_signal(barrier, inc=1, device_id=(p, partner), device_id_type=MESH)
 
-    for b in range(2):
-        code[p, b] = jnp.exp(CODE * mask_ref[0, :, b * h : (b + 1) * h]).astype(BF16)
+    def encode(half, which):
+        here = rows_of(which)
+        cols = pl.ds(pl.multiple_of(half * h, h), h)
+        code[p, half, here] = quarter_tan(mask_ref[0, here, cols]).astype(BF16)
+
+    encode(core, chip)
     pl.semaphore_wait(barrier, planes - 1 + chips - 1 + 1)
 
     for step in range(1, planes):
         mask_z(step).start()
 
-    make_operators(n, left, right, prop)
+    encode(1 - core, chip)
+    for step in range(1, chips):
+        for half in range(2):
+            encode(half, at_chip(step))
+    make_operators(n, left, right)
 
     def spread_layer(k):
         @pl.when(p != k)
@@ -226,7 +260,7 @@
         spread_layer(k)
 
     make_tables(
-        n, orders_ref[0, p], orders_ref[1, p], spots_ref[p], prop, row_tab, col_tab
+        n, orders_ref[0, p], orders_ref[1, p], spots_ref[p], right, row_tab, col_tab
     )
     spread_core(0)
 
@@ -289,8 +323,7 @@
                 field_re, field_im = combined(i)
             masked_re, masked_im = {}, {}
             for a, b in quads:
-                phase = jnp.log(code[k, b, span(i, a)].astype(F32)) * (1.0 / CODE)
-                s, c = sincos(phase)
+                s, c = sincos_of(code[k, b, span(i, a)].astype(F32))
                 cosm[k, b, span(i, a)] = c
                 sinm[k, b, span(i, a)] = s
                 if field_im is None:
@@ -460,7 +493,6 @@
             vmem((2, n, n), F32),
             vmem((2, n, n), BF16),
             vmem((2, n, n), BF16),
-            vmem((2, 2, h, h), F32),
             vmem((8, n), F32),
             vmem((n, 128), F32),
             vmem((planes, 2, n, h), BF16),

time: 67.2 us -> 65.5 us (0.975)
  Pallas kernels: 65.4 us -> 63.7 us
    pallas_call x1, Pallas kernels: 65.4 us -> 63.7 us  [shards(): pl.pallas_call(functools.partial(kernel, planes, modes), out_shape=jax.Sh...]
where the time goes in v3:
time: 65.5 us; the launch traced here: 65.3 us
  Pallas kernels  63.7 us (97%)
  local copies, waits for them, and re-layouts  1.67 us (3%)
    pallas_call x1, Pallas kernels, shards(): pl.pallas_call(functools.partial(kernel, planes, modes), out_shape=jax.Sh...  63.7 us
    unnamed x5, local copies, waits for them, and re-layouts  1.67 us

profile of v3, /device:TPU:1, one launch (start us, length us, event | category | flops | bytes accessed | tf_op | source)
XLA Modules:
  0.0 65.3 jit_solution(17802750638163669413)
XLA Ops:
  0.0 0.0 copy-start.1
  0.0 0.0 copy-start
  0.0 0.7 copy-done.1
  0.7 0.0 copy-done
  0.7 63.7 %phase_update.1 = f32[1,512,512]{2,1,0:T(8,128)S(1)} custom-call(s32[2,4]{1,0:T(2,128)S(1)} %bitcast.1, s32[4]{0:T(128)S(1)} %copy-done.1, f32[1,512,512]{2,1,0:T(8,128)} %mask_ref.1), custom_call_target="tpu_custom_call" | custom-call | tf_op jit(solution)/shard_map/phase_update/pallas_call | solution.py:476
  64.4 1.0 %copy.5 = f32[1,512,512]{2,1,0:T(8,128)} copy(f32[1,512,512]{2,1,0:T(8,128)S(1)} %phase_update.1) | data formatting | bytes 2097152
Async XLA Ops:
  0.0 0.7 %copy-start.1 = (s32[4]{0:T(128)S(1)}, s32[4]{0:T(128)}, u32[]{:S(2)}) copy-start(s32[4]{0:T(128)} %spots_ref.1) | copy-start | bytes 52
  0.0 0.7 %copy-start = (s32[4,2]{0,1:T(2,128)S(1)}, s32[4,2]{0,1:T(2,128)}, u32[]{:S(2)}) copy-start(s32[4,2]{0,1:T(2,128)} %param.4) | copy-start | bytes 100

commit v4 on v3

--- a/solution.py
+++ b/solution.py
@@ -14,6 +14,7 @@
 AMPLITUDE = 12.0
 EPSILON = 1e-06
 CHUNK = 16
+STRIP = 128
 F32 = jnp.float32
 BF16 = jnp.bfloat16
 MESH = pl.DeviceIdType.MESH
@@ -188,31 +189,45 @@
     def mask_core(k):
         return remote(code.at[k, core], code.at[k, core], mc_s.at[k], mc_r.at[k], mode=partner)
 
-    def grad_a(k):
-        return remote(grad.at[k, 1 - core], in_a.at[k], a_s.at[k], a_r.at[k], mode=partner)
-
-    def grad_b(k, step):
+    parts = in_b.shape[2]
+    size = rows // parts
+
+    def part_rows(which, q):
+        return pl.ds(pl.multiple_of(q * (n // parts) + which * size, size), size)
+
+    def half_rows(q):
+        return pl.ds(q * (n // parts), n // parts)
+
+    def grad_a(k, q):
+        return remote(
+            grad.at[k, 1 - core, half_rows(q)], in_a.at[k, half_rows(q)],
+            a_s.at[k, q], a_r.at[k, q], mode=partner,
+        )
+
+    def grad_b(k, q, step):
         there = at_chip(step)
         return remote(
-            sum_a.at[k, rows_of(there)], in_b.at[k, step - 1], b_s.at[k, step - 1],
-            b_r.at[k, step - 1], mode=there * 2 + core,
-        )
-
-    def grad_c(k):
-        return remote(piece.at[k], in_c.at[p], c_s.at[k], c_r.at[p], plane=k)
-
-    def grad_c_in(source):
-        return remote(piece.at[0], in_c.at[source], c_s.at[0], c_r.at[source], plane=source)
-
-    def grad_d(step):
-        spot = final.at[core, mine]
+            sum_a.at[k, part_rows(there, q)], in_b.at[k, step - 1, q], b_s.at[k, q, step - 1],
+            b_r.at[k, q, step - 1], mode=there * 2 + core,
+        )
+
+    def grad_c(k, q):
+        return remote(piece.at[k, q], in_c.at[p, q], c_s.at[k, q], c_r.at[p, q], plane=k)
+
+    def grad_c_in(source, q):
         return remote(
-            spot, spot, d_s.at[step - 1], d_r.at[step - 1], mode=at_chip(step) * 2 + core
-        )
-
-    def grad_e(step):
-        spot = final.at[core, rows_of(at_chip(chips - step))]
-        return remote(spot, spot, e_s.at[step], e_r.at[step], mode=partner)
+            piece.at[0, q], in_c.at[source, q], c_s.at[0, q], c_r.at[source, q], plane=source
+        )
+
+    def grad_d(q, step):
+        spot = final.at[core, part_rows(chip, q)]
+        return remote(
+            spot, spot, d_s.at[q, step - 1], d_r.at[q, step - 1], mode=at_chip(step) * 2 + core
+        )
+
+    def grad_e(q, step):
+        spot = final.at[core, part_rows(at_chip(chips - step), q)]
+        return remote(spot, spot, e_s.at[q, step], e_r.at[q, step], mode=partner)
 
     barrier = pltpu.get_barrier_semaphore()
     for step in range(1, planes):
@@ -277,15 +292,20 @@
             (1, 0): top - bottom, (1, 1): top_d - bottom_d,
         }
 
-    def combined(i):
-        re = hadamard({(a, b): y_buf[b, span(i, a), :h] for a, b in quads})
-        im = hadamard({(a, b): y_buf[b, span(i, a), h:] for a, b in quads})
+    strips = [slice(at, at + STRIP) for at in range(0, h, STRIP)]
+
+    def columns(strip, b):
+        return slice(b * h + strip.start, b * h + strip.stop)
+
+    def combined(i, strip):
+        re = hadamard({(a, b): y_buf[b, span(i, a), columns(strip, 0)] for a, b in quads})
+        im = hadamard({(a, b): y_buf[b, span(i, a), columns(strip, 1)] for a, b in quads})
         return re, im
 
-    def put_sums(i, re, im):
+    def put_sums(i, strip, re, im):
         for part, q in enumerate((hadamard(re), hadamard(im))):
             for a, b in quads:
-                x_buf[a, span(i, part), b * h : (b + 1) * h] = q[a, b].astype(BF16)
+                x_buf[a, span(i, part), columns(strip, b)] = q[a, b].astype(BF16)
 
     def products(first, second):
         for a in range(2):
@@ -298,9 +318,9 @@
         for b in range(2):
             y_buf[b] = jnp.dot(w_buf[b], second[b], preferred_element_type=F32)
 
-    def outer(i, a, b):
+    def outer(i, strip, a, b):
         ar, ai = col_tab[span(i, a), 2:3], col_tab[span(i, a), 3:4]
-        br, bi = row_tab[4:5, b * h : (b + 1) * h], row_tab[5:6, b * h : (b + 1) * h]
+        br, bi = row_tab[4:5, columns(strip, b)], row_tab[5:6, columns(strip, b)]
         return ar * br - ai * bi, ar * bi + ai * br
 
     for k in range(planes):
@@ -313,39 +333,44 @@
         last = k == planes - 1
 
         def forward(i, carry):
+            for strip in strips:
+                carry = forward_strip(i, strip, carry)
+            return carry
+
+        def forward_strip(i, strip, carry):
             if k == 0:
                 field_re = {
-                    (a, b): col_tab[span(i, a), 0:1] * row_tab[1:2, b * h : (b + 1) * h]
+                    (a, b): col_tab[span(i, a), 0:1] * row_tab[1:2, columns(strip, b)]
                     for a, b in quads
                 }
                 field_im = None
             else:
-                field_re, field_im = combined(i)
+                field_re, field_im = combined(i, strip)
             masked_re, masked_im = {}, {}
             for a, b in quads:
-                s, c = sincos_of(code[k, b, span(i, a)].astype(F32))
-                cosm[k, b, span(i, a)] = c
-                sinm[k, b, span(i, a)] = s
+                s, c = sincos_of(code[k, b, span(i, a), strip].astype(F32))
+                cosm[k, b, span(i, a), strip] = c
+                sinm[k, b, span(i, a), strip] = s
                 if field_im is None:
                     re, im = field_re[a, b] * c, field_re[a, b] * s
                 else:
                     fr, fi = field_re[a, b], field_im[a, b]
                     re, im = fr * c - fi * s, fr * s + fi * c
                 masked_re[a, b], masked_im[a, b] = re, im
-                g_re[k, b, span(i, a)] = re.astype(BF16)
-                g_im[k, b, span(i, a)] = im.astype(BF16)
+                g_re[k, b, span(i, a), strip] = re.astype(BF16)
+                g_im[k, b, span(i, a), strip] = im.astype(BF16)
             if not last:
-                put_sums(i, masked_re, masked_im)
+                put_sums(i, strip, masked_re, masked_im)
                 return carry
             total_re, total_im = carry
             for a, b in quads:
-                er, ei = outer(i, a, b)
+                er, ei = outer(i, strip, a, b)
                 re, im = masked_re[a, b], masked_im[a, b]
                 total_re += er * re - ei * im
                 total_im += er * im + ei * re
             return total_re, total_im
 
-        zero = jnp.zeros((CHUNK, h), F32)
+        zero = jnp.zeros((CHUNK, STRIP), F32)
         totals = lax.fori_loop(0, h // CHUNK, forward, (zero, zero) if last else 0)
         if not last:
             spread_core(k + 1)
@@ -353,77 +378,89 @@
     coupling_re = jnp.sum(totals[0], keepdims=True)
     coupling_im = jnp.sum(totals[1], keepdims=True)
 
-    def settle_a(k):
-        grad_a(k).wait_recv()
-        sum_a[k] = (grad[k, core].astype(F32) + in_a[k].astype(F32)).astype(BF16)
+    def settle_a(k, q):
+        grad_a(k, q).wait_recv()
+        here = half_rows(q)
+        sum_a[k, here] = (grad[k, core, here].astype(F32) + in_a[k, here].astype(F32)).astype(BF16)
         for step in range(1, chips):
-            grad_b(k, step).start()
-
-    def settle_b(k):
+            grad_b(k, q, step).start()
+
+    def settle_b(k, q):
         for step in range(1, chips):
-            grad_b(k, step).wait_recv()
-        total = sum_a[k, mine].astype(F32)
+            grad_b(k, q, step).wait_recv()
+        total = sum_a[k, part_rows(chip, q)].astype(F32)
         for step in range(1, chips):
-            total += in_b[k, step - 1].astype(F32)
-        piece[k] = total.astype(BF16)
+            total += in_b[k, step - 1, q].astype(F32)
+        piece[k, q] = total.astype(BF16)
 
         @pl.when(p != k)
         def _():
-            grad_c(k).start()
+            grad_c(k, q).start()
 
         @pl.when(p == k)
         def _():
-            in_c[k] = piece[k]
+            in_c[k, q] = piece[k, q]
 
     for k in range(planes - 1, -1, -1):
         def backward(i, carry):
+            for strip in strips:
+                backward_strip(i, strip)
+            return carry
+
+        def backward_strip(i, strip):
             if k == planes - 1:
                 back_re, back_im = {}, {}
                 for a, b in quads:
-                    er, ei = outer(i, a, b)
+                    er, ei = outer(i, strip, a, b)
                     back_re[a, b] = coupling_re * er + coupling_im * ei
                     back_im[a, b] = coupling_im * er - coupling_re * ei
             else:
-                back_re, back_im = combined(i)
+                back_re, back_im = combined(i, strip)
             reply_re, reply_im = {}, {}
             for a, b in quads:
                 br, bi = back_re[a, b], back_im[a, b]
-                gr = g_re[k, b, span(i, a)].astype(F32)
-                gi = g_im[k, b, span(i, a)].astype(F32)
-                grad[k, b, span(i, a)] = (2.0 * (bi * gr - br * gi)).astype(BF16)
+                gr = g_re[k, b, span(i, a), strip].astype(F32)
+                gi = g_im[k, b, span(i, a), strip].astype(F32)
+                grad[k, b, span(i, a), strip] = (2.0 * (bi * gr - br * gi)).astype(BF16)
                 if k > 0:
-                    c, s = cosm[k, b, span(i, a)], sinm[k, b, span(i, a)]
+                    c, s = cosm[k, b, span(i, a), strip], sinm[k, b, span(i, a), strip]
                     reply_re[a, b] = br * c + bi * s
                     reply_im[a, b] = bi * c - br * s
             if k > 0:
-                put_sums(i, reply_re, reply_im)
-            return carry
+                put_sums(i, strip, reply_re, reply_im)
 
         lax.fori_loop(0, h // CHUNK, backward, 0)
-        grad_a(k).start()
+        for q in range(parts):
+            grad_a(k, q).start()
         if k > 0:
             products(right, left)
-        if k + 1 < planes:
-            settle_b(k + 1)
-        settle_a(k)
-    settle_b(0)
-
-    for k in range(planes):
-        @pl.when(p != k)
-        def _():
-            grad_c_in(k).wait_recv()
-    total = in_c[0].astype(F32)
-    for k in range(1, planes):
-        total += in_c[k].astype(F32)
-    final[core, mine] = total.astype(BF16)
-    for step in range(1, chips):
-        grad_d(step).start()
-    grad_e(0).start()
-    for step in range(1, chips):
-        grad_d(step).wait_recv()
-        grad_e(step).start()
-    for step in range(chips):
-        grad_e(step).wait_recv()
+        for q in range(parts):
+            if k + 1 < planes:
+                settle_b(k + 1, q)
+        for q in range(parts):
+            settle_a(k, q)
+    for q in range(parts):
+        settle_b(0, q)
+
+    for q in range(parts):
+        for k in range(planes):
+            @pl.when(p != k)
+            def _():
+                grad_c_in(k, q).wait_recv()
+        total = in_c[0, q].astype(F32)
+        for k in range(1, planes):
+            total += in_c[k, q].astype(F32)
+        final[core, part_rows(chip, q)] = total.astype(BF16)
+        for step in range(1, chips):
+            grad_d(q, step).start()
+        grad_e(q, 0).start()
+    for q in range(parts):
+        for step in range(1, chips):
+            grad_d(q, step).wait_recv()
+            grad_e(q, step).start()
+    for q in range(parts):
+        for step in range(chips):
+            grad_e(q, step).wait_recv()
 
     def square(i, carry):
         here = pl.ds(pl.multiple_of(i * CHUNK, CHUNK), CHUNK)
@@ -453,15 +490,18 @@
             for step in range(1, chips):
                 mask_layer(k, step).wait_send()
             mask_core(k).wait_send()
-            grad_c(k).wait_send()
-
-        grad_a(k).wait_send()
+            for q in range(parts):
+                grad_c(k, q).wait_send()
+
+        for q in range(parts):
+            grad_a(k, q).wait_send()
+            for step in range(1, chips):
+                grad_b(k, q, step).wait_send()
+    for q in range(parts):
         for step in range(1, chips):
-            grad_b(k, step).wait_send()
-    for step in range(1, chips):
-        grad_d(step).wait_send()
-    for step in range(chips):
-        grad_e(step).wait_send()
+            grad_d(q, step).wait_send()
+        for step in range(chips):
+            grad_e(q, step).wait_send()
 
 
 def shards(planes, modes, phase_masks, hg_orders, spot_index):
@@ -470,6 +510,7 @@
     chips = modes // 2
     rows = n // chips
     others = max(chips - 1, 1)
+    parts = 2 if rows % 32 == 0 else 1
     assert hg_orders.shape[0] == planes and n & (n - 1) == 0
     dma = pltpu.SemaphoreType.DMA
     vmem = pltpu.VMEM
@@ -498,18 +539,18 @@
             vmem((planes, 2, n, h), BF16),
             vmem((planes, n, h), BF16),
             vmem((planes, n, h), BF16),
-            vmem((planes, others, rows, h), BF16),
-            vmem((planes, rows, h), BF16),
-            vmem((planes, rows, h), BF16),
+            vmem((planes, others, parts, rows // parts, h), BF16),
+            vmem((planes, parts, rows // parts, h), BF16),
+            vmem((planes, parts, rows // parts, h), BF16),
             vmem((2, n, h), BF16),
             dma((max(planes - 1, 1),)), dma((planes,)),
             dma((planes, others)), dma((planes, others)),
             dma((planes,)), dma((planes,)),
-            dma((planes,)), dma((planes,)),
-            dma((planes, others)), dma((planes, others)),
-            dma((planes,)), dma((planes,)),
-            dma((others,)), dma((others,)),
-            dma((chips,)), dma((chips,)),
+            dma((planes, parts)), dma((planes, parts)),
+            dma((planes, parts, others)), dma((planes, parts, others)),
+            dma((planes, parts)), dma((planes, parts)),
+            dma((parts, others)), dma((parts, others)),
+            dma((parts, chips)), dma((parts, chips)),
         ],
         compiler_params=pltpu.CompilerParams(
             collective_id=0, has_side_effects=True, vmem_limit_bytes=52 * 1024 * 1024

time: 65.5 us -> 64.9 us (level)
  no operation moved by 1% of the time
where the time goes in v4:
time: 64.9 us; the launch traced here: 64.7 us
  Pallas kernels  63.1 us (97%)
  local copies, waits for them, and re-layouts  1.67 us (3%)
    pallas_call x1, Pallas kernels, shards(): pl.pallas_call(functools.partial(kernel, planes, modes), out_shape=jax.Sh...  63.1 us
    unnamed x5, local copies, waits for them, and re-layouts  1.67 us

profile of v4, /device:TPU:1, one launch (start us, length us, event | category | flops | bytes accessed | tf_op | source)
XLA Modules:
  0.0 64.7 jit_solution(9883150525538096075)
XLA Ops:
  0.0 0.0 copy-start.1
  0.0 0.0 copy-start
  0.0 0.7 %copy-done.1 = s32[4]{0:T(128)S(1)} copy-done((s32[4]{0:T(128)S(1)}, s32[4]{0:T(128)}, u32[]{:S(2)}) %copy-start.1) | copy-done | bytes 40
  0.7 0.0 copy-done
  0.7 63.1 %phase_update.1 = f32[1,512,512]{2,1,0:T(8,128)S(1)} custom-call(s32[2,4]{1,0:T(2,128)S(1)} %bitcast.1, s32[4]{0:T(128)S(1)} %copy-done.1, f32[1,512,512]{2,1,0:T(8,128)} %mask_ref.1), custom_call_target="tpu_custom_call" | custom-call | tf_op jit(solution)/shard_map/phase_update/pallas_call | solution.py:517
  63.8 1.0 %copy.5 = f32[1,512,512]{2,1,0:T(8,128)} copy(f32[1,512,512]{2,1,0:T(8,128)S(1)} %phase_update.1) | data formatting | bytes 2097152
Async XLA Ops:
  0.0 0.7 %copy-start.1 = (s32[4]{0:T(128)S(1)}, s32[4]{0:T(128)}, u32[]{:S(2)}) copy-start(s32[4]{0:T(128)} %spots_ref.1) | copy-start | bytes 52
  0.0 0.7 %copy-start = (s32[4,2]{0,1:T(2,128)S(1)}, s32[4,2]{0,1:T(2,128)}, u32[]{:S(2)}) copy-start(s32[4,2]{0,1:T(2,128)} %param.4) | copy-start | bytes 100

commit v5 on v4

--- a/solution.py
+++ b/solution.py
@@ -248,8 +248,10 @@
     encode(core, chip)
     pl.semaphore_wait(barrier, planes - 1 + chips - 1 + 1)
 
-    for step in range(1, planes):
-        mask_z(step).start()
+    for step in range(planes - 1, 0, -1):
+        @pl.when((p == 0) | (p + step >= planes))
+        def _():
+            mask_z(step).start()
 
     encode(1 - core, chip)
     for step in range(1, chips):
@@ -264,6 +266,12 @@
             for step in range(1, chips):
                 mask_layer(k, step).start()
 
+        if k == 0:
+            for step in range(planes - 1, 0, -1):
+                @pl.when((p > 0) & (p + step < planes))
+                def _():
+                    mask_z(step).start()
+
     def spread_core(k):
         @pl.when(p != k)
         def _():
@@ -271,9 +279,10 @@
                 mask_layer(k, step).wait_recv()
             mask_core(k).start()
 
-    for k in range(min(2, planes)):
-        spread_layer(k)
-
+        if k + 1 < planes:
+            spread_layer(k + 1)
+
+    spread_layer(0)
     make_tables(
         n, orders_ref[0, p], orders_ref[1, p], spots_ref[p], right, row_tab, col_tab
     )
@@ -307,7 +316,7 @@
             for a, b in quads:
                 x_buf[a, span(i, part), columns(strip, b)] = q[a, b].astype(BF16)
 
-    def products(first, second):
+    def products(first, second, between=None):
         for a in range(2):
             v = jnp.dot(first[a], x_buf[a], preferred_element_type=F32)
             for b in range(2):
@@ -315,6 +324,8 @@
                     w_buf[b, a * h : (a + 1) * h, part * h : (part + 1) * h] = v[
                         part * h : (part + 1) * h, b * h : (b + 1) * h
                     ].astype(BF16)
+        if between is not None:
+            between()
         for b in range(2):
             y_buf[b] = jnp.dot(w_buf[b], second[b], preferred_element_type=F32)
 
@@ -328,8 +339,6 @@
         def _():
             mask_core(k).wait_recv()
 
-        if k + 2 < planes:
-            spread_layer(k + 2)
         last = k == planes - 1
 
         def forward(i, carry):
@@ -373,8 +382,7 @@
         zero = jnp.zeros((CHUNK, STRIP), F32)
         totals = lax.fori_loop(0, h // CHUNK, forward, (zero, zero) if last else 0)
         if not last:
-            spread_core(k + 1)
-            products(left, right)
+            products(left, right, functools.partial(spread_core, k + 1))
     coupling_re = jnp.sum(totals[0], keepdims=True)
     coupling_im = jnp.sum(totals[1], keepdims=True)
 

time: 64.9 us -> 67.8 us (1.045)
  Pallas kernels: 63.1 us -> 65.9 us
    pallas_call x1, Pallas kernels: 63.1 us -> 65.9 us  [shards(): pl.pallas_call(functools.partial(kernel, planes, modes), out_shape=jax.Sh...]
where the time goes in v5:
time: 67.8 us; the launch traced here: 67.6 us
  Pallas kernels  65.9 us (97%)
  local copies, waits for them, and re-layouts  1.67 us (2%)
    pallas_call x1, Pallas kernels, shards(): pl.pallas_call(functools.partial(kernel, planes, modes), out_shape=jax.Sh...  65.9 us
    unnamed x5, local copies, waits for them, and re-layouts  1.67 us

profile of v5, /device:TPU:1, one launch (start us, length us, event | category | flops | bytes accessed | tf_op | source)
XLA Modules:
  0.0 67.6 jit_solution(18190324790507357280)
XLA Ops:
  0.0 0.0 copy-start.1
  0.0 0.0 copy-start
  0.0 0.7 copy-done.1
  0.7 0.0 copy-done
  0.7 65.9 %phase_update.1 = f32[1,512,512]{2,1,0:T(8,128)S(1)} custom-call(s32[2,4]{1,0:T(2,128)S(1)} %bitcast.1, s32[4]{0:T(128)S(1)} %copy-done.1, f32[1,512,512]{2,1,0:T(8,128)} %mask_ref.1), custom_call_target="tpu_custom_call" | custom-call | tf_op jit(solution)/shard_map/phase_update/pallas_call | solution.py:525
  66.6 1.0 %copy.5 = f32[1,512,512]{2,1,0:T(8,128)} copy(f32[1,512,512]{2,1,0:T(8,128)S(1)} %phase_update.1) | data formatting | bytes 2097152
Async XLA Ops:
  0.0 0.7 copy-start.1
  0.0 0.7 %copy-start = (s32[4,2]{0,1:T(2,128)S(1)}, s32[4,2]{0,1:T(2,128)}, u32[]{:S(2)}) copy-start(s32[4,2]{0,1:T(2,128)} %param.4) | copy-start | bytes 100

commit v6 on v4

--- a/solution.py
+++ b/solution.py
@@ -248,7 +248,7 @@
     encode(core, chip)
     pl.semaphore_wait(barrier, planes - 1 + chips - 1 + 1)
 
-    for step in range(1, planes):
+    for step in range(planes - 1, 0, -1):
         mask_z(step).start()
 
     encode(1 - core, chip)
@@ -277,6 +277,8 @@
     make_tables(
         n, orders_ref[0, p], orders_ref[1, p], spots_ref[p], right, row_tab, col_tab
     )
+    for k in range(2, planes):
+        spread_layer(k)
     spread_core(0)
 
     quads = [(a, b) for a in range(2) for b in range(2)]
@@ -328,8 +330,6 @@
         def _():
             mask_core(k).wait_recv()
 
-        if k + 2 < planes:
-            spread_layer(k + 2)
         last = k == planes - 1
 
         def forward(i, carry):

time: 64.9 us -> 65.2 us (level)
  no operation moved by 1% of the time
where the time goes in v6:
time: 65.2 us; the launch traced here: 65 us
  Pallas kernels  63.3 us (97%)
  local copies, waits for them, and re-layouts  1.67 us (3%)
    pallas_call x1, Pallas kernels, shards(): pl.pallas_call(functools.partial(kernel, planes, modes), out_shape=jax.Sh...  63.3 us
    unnamed x5, local copies, waits for them, and re-layouts  1.67 us

profile of v6, /device:TPU:1, one launch (start us, length us, event | category | flops | bytes accessed | tf_op | source)
XLA Modules:
  0.0 65.0 jit_solution(5364348425733352700)
XLA Ops:
  0.0 0.0 copy-start.1
  0.0 0.0 copy-start
  0.0 0.7 %copy-done.1 = s32[4]{0:T(128)S(1)} copy-done((s32[4]{0:T(128)S(1)}, s32[4]{0:T(128)}, u32[]{:S(2)}) %copy-start.1) | copy-done | bytes 40
  0.7 0.0 copy-done
  0.7 63.3 %phase_update.1 = f32[1,512,512]{2,1,0:T(8,128)S(1)} custom-call(s32[2,4]{1,0:T(2,128)S(1)} %bitcast.1, s32[4]{0:T(128)S(1)} %copy-done.1, f32[1,512,512]{2,1,0:T(8,128)} %mask_ref.1), custom_call_target="tpu_custom_call" | custom-call | tf_op jit(solution)/shard_map/phase_update/pallas_call | solution.py:517
  64.0 1.0 %copy.5 = f32[1,512,512]{2,1,0:T(8,128)} copy(f32[1,512,512]{2,1,0:T(8,128)S(1)} %phase_update.1) | data formatting | bytes 2097152
Async XLA Ops:
  0.0 0.7 %copy-start.1 = (s32[4]{0:T(128)S(1)}, s32[4]{0:T(128)}, u32[]{:S(2)}) copy-start(s32[4]{0:T(128)} %spots_ref.1) | copy-start | bytes 52
  0.0 0.7 %copy-start = (s32[4,2]{0,1:T(2,128)S(1)}, s32[4,2]{0,1:T(2,128)}, u32[]{:S(2)}) copy-start(s32[4,2]{0,1:T(2,128)} %param.4) | copy-start | bytes 100
